TPU v7x, 32 devices: a whole 2x2x4 slice. The times are simulated.
32 devices in a mesh: rep: 2 (over y), row: 8 (over z, core), col: 2 (over x).
Axes of the slice: x: 2, y: 2, z: 4, core: 2. Of those that a mesh axis runs over, the one named last changes fastest.
Arguments:
- pair: bfloat16 [448, 224, 128], P(('rep', 'row'), 'col'), parts along dimension 0, may hold values from -6 to 6
- tri_gains: float32 [2, 2, 128], replicated, may hold values from 0.25 to 1.75
- tri_proj: bfloat16 [2, 5, 128, 128], replicated, may hold values from -0.5 to 0.5
- tri_out: bfloat16 [2, 128, 128], replicated, may hold values from -0.5 to 0.5
- trans_gain: float32 [128], replicated, may hold values from 0.25 to 1.75
- trans_up: bfloat16 [2, 128, 512], replicated, may hold values from -0.5 to 0.5
- trans_down: bfloat16 [512, 128], replicated, may hold values from -0.25 to 0.25
Outputs:
- pair_out: bfloat16 [448, 224, 128], P(('rep', 'row'), 'col'), parts along dimension 0
There are 2 independent parts, one for each index of `rep`. A program takes and returns all parts, laid end to end along the dimension named above; an argument that names none is the same for every part. Nothing has to cross between parts.
All inputs are finite; a program needn't handle non-finite values.
Results may differ from a plain program's by a relative error of at most 0.018.
Values may be sent and summed in bfloat16 or wider, within the bound.
A program may use at most 128 MiB of HBM per device.

v0:
```python
import jax
import jax.numpy as jnp
from jax import lax
from jax.sharding import PartitionSpec as P


def normalize(values, gain):
    mean = jnp.mean(values, axis=-1, keepdims=True)
    centered = values - mean
    variance = jnp.mean(centered * centered, axis=-1, keepdims=True)
    return centered * lax.rsqrt(variance + 1e-05) * gain


def project(flat, weight):
    return jnp.dot(flat, weight, preferred_element_type=jnp.float32)


def prepare(pair, gains, weights):
    rows, cols, width = pair.shape
    flat = normalize(pair.reshape(-1, width).astype(jnp.float32), gains[0]).astype(jnp.bfloat16)
    left = (jax.nn.sigmoid(project(flat, weights[1])) * project(flat, weights[0])).astype(
        jnp.bfloat16
    )
    right = (jax.nn.sigmoid(project(flat, weights[3])) * project(flat, weights[2])).astype(
        jnp.bfloat16
    )
    gate = jax.nn.sigmoid(project(flat, weights[4]))
    return (left.reshape(rows, cols, width), right.reshape(rows, cols, width), gate)


def finish(pair, summed, gate, gains, weight):
    width = pair.shape[2]
    flat = normalize(summed.reshape(-1, width), gains[1]).astype(jnp.bfloat16)
    result = pair.reshape(-1, width).astype(jnp.float32) + gate * project(flat, weight)
    return result.astype(jnp.bfloat16).reshape(pair.shape)


def incoming_fold(right, left_cols):
    return jnp.einsum(
        "kic,kjc->ijc",
        left_cols,
        lax.all_gather(right, "row", axis=0, tiled=True),
        preferred_element_type=jnp.float32,
    )


def on_device(pair, tri_gains, tri_proj, tri_out, trans_gain, trans_up, trans_down):
    rows, cols, width = pair.shape
    left, right, gate = prepare(pair, tri_gains[0], tri_proj[0])
    right_every = lax.all_gather(right, "row", axis=0, tiled=True)
    swapped = lax.psum_scatter(
        jnp.einsum("jkc,ikc->jic", right_every, left, preferred_element_type=jnp.float32).astype(
            jnp.bfloat16
        ),
        "col",
        scatter_dimension=0,
        tiled=True,
    ).astype(jnp.float32)
    summed = jnp.transpose(swapped, (1, 0, 2))
    pair_mid = finish(pair, summed, gate, tri_gains[0], tri_out[0])
    left, right, gate = prepare(pair_mid, tri_gains[1], tri_proj[1])
    panel_left = lax.all_gather(left, "col", axis=1, tiled=True)
    left_cols = lax.all_to_all(panel_left, "row", split_axis=1, concat_axis=0, tiled=True)
    summed = incoming_fold(right, left_cols)
    pair_new = finish(pair_mid, summed, gate, tri_gains[1], tri_out[1])
    flat = normalize(pair_new.reshape(-1, width).astype(jnp.float32), trans_gain).astype(
        jnp.bfloat16
    )
    inner = (jax.nn.silu(project(flat, trans_up[0])) * project(flat, trans_up[1])).astype(
        jnp.bfloat16
    )
    result = pair_new.reshape(-1, width).astype(jnp.float32) + project(inner, trans_down)
    return result.astype(jnp.bfloat16).reshape(rows, cols, width)


def solution(mesh):
    placed = (P(("rep", "row"), "col", None), P(), P(), P(), P(), P(), P())
    return jax.shard_map(
        on_device,
        mesh=mesh,
        in_specs=placed,
        out_specs=P(("rep", "row"), "col", None),
        check_vma=False,
    )
```

profile of v0, /device:TPU:0, one launch (start us, length us, event | category | flops | bytes accessed | tf_op | source)
XLA Modules:
  0.0 317.3 jit_solution(7953137321949633885)
XLA Ops:
  6.5 0.0 copy-start
  6.5 0.0 copy-start.1
  6.5 0.0 all-gather.4.cloned.1.call-start
  6.5 0.8 slice_bitcast_fusion
  7.4 1.5 convert_reduce_fusion
  8.9 2.1 multiply_reduce_fusion.3
  11.0 0.0 copy-done.1
  11.0 1.0 multiply_convert_fusion.3
  12.1 0.0 copy-done.6
  12.1 0.6 fusion.14
  12.7 1.2 fusion.22
  13.9 0.0 all-gather.4.cloned.1.call-update
  13.9 0.0 reduce-scatter.2.cloned.1.call-start
  14.0 0.6 fusion.17
  14.6 0.3 fusion.21
  14.9 2.2 copy.29
  17.1 65.5 %all-gather.4.cloned.1.call-done = bf16[224,112,128]{2,1,0:T(8,128)(2,1)} async-done(((bf16[28,112,128]{2,1,0:T(8,128)(2,1)}), bf16[224,112,128]{2,1,0:T(8,128)(2,1)}) %all-gather.4.cloned.1.call-update) | async-done | bytes 6422544 | tf_op jit(solution)/shard_map/all_gather | solution.py:50
  82.6 10.1 %copy.30 = bf16[224,112,128]{1,0,2:T(8,128)(2,1)} copy(bf16[224,112,128]{2,1,0:T(8,128)(2,1)} %all-gather.4.cloned.1.call-done) | data formatting | bytes 12845056 | tf_op jit(solution)/shard_map/all_gather | solution.py:50
  92.8 9.1 %convert_bitcast_fusion = bf16[224,28,128]{0,1,2:T(8,128)(2,1)} fusion(bf16[28,112,128]{1,0,2:T(8,128)(2,1)} %copy.29, bf16[224,112,128]{1,0,2:T(8,128)(2,1)} %copy.30), kind=kOutput, calls=%fused_computation.48 | convolution fusion | flops 180633600 | bytes 8830976 | tf_op jit(solution)/shard_map/jkc,ikc->jic/dot_general | solution.py:52
  101.9 4.8 %copy.31 = bf16[224,28,128]{2,1,0:T(8,128)(2,1)} copy(bf16[224,28,128]{0,1,2:T(8,128)(2,1)} %convert_bitcast_fusion) | data formatting | bytes 3211264 | tf_op jit(solution)/shard_map/convert_element_type | solution.py:52
  106.7 0.0 reduce-scatter.2.cloned.1.call-update
  106.7 0.2 all-gather.8.cloned.1.call-start
  107.0 1.7 fusion.20
  108.7 25.8 %reduce-scatter.2.cloned.1.call-done = bf16[112,28,128]{2,1,0:T(8,128)(2,1)} async-done(((bf16[224,28,128]{2,1,0:T(8,128)(2,1)}), bf16[112,28,128]{2,1,0:T(8,128)(2,1)}) %reduce-scatter.2.cloned.1.call-update) | async-done | bytes 802832 | tf_op jit(solution)/shard_map/reduce_scatter | solution.py:51
  134.5 1.8 bitcast_reduce_fusion.1
  136.3 0.0 copy-start.3
  136.3 0.0 copy-start.5
  136.3 2.3 fusion.32
  138.6 0.0 copy-done.2
  138.6 1.3 fusion.34
  140.0 0.0 copy-done.3
  140.0 0.0 copy-done.5
  140.0 0.7 fusion.73
  140.7 0.9 multiply_reduce_fusion.2
  141.7 1.7 multiply_convert_fusion.2
  143.4 0.6 fusion.5
  144.0 1.2 fusion.26
  145.2 0.0 all-gather.8.cloned.1.call-update
  145.2 0.0 all-gather.6.cloned.1.call-start
  145.3 0.6 fusion.8
  145.9 1.2 fusion.25
  147.1 0.0 all-gather.6.cloned.1.call-update
  147.1 25.9 %all-gather.8.cloned.1.call-done = bf16[28,224,128]{2,1,0:T(8,128)(2,1)} async-done(((bf16[28,112,128]{2,1,0:T(8,128)(2,1)}), bf16[28,224,128]{2,1,0:T(8,128)(2,1)}) %all-gather.8.cloned.1.call-update) | async-done | bytes 1605648 | tf_op jit(solution)/shard_map/all_gather | solution.py:62
  173.0 3.3 %copy.33 = bf16[28,224,128]{2,0,1:T(8,128)(2,1)} copy(bf16[28,224,128]{2,1,0:T(8,128)(2,1)} %all-gather.8.cloned.1.call-done) | data formatting | bytes 3211264 | tf_op jit(solution)/shard_map/all_gather | solution.py:62
  176.3 4.6 %all-to-all-start = ((bf16[28,224,128]{2,0,1:T(8,128)(2,1)}), bf16[28,224,128]{2,0,1:T(8,128)(2,1)}, u32[]{:S(2)}, u32[]{:S(2)}) async-start(bf16[28,224,128]{2,0,1:T(8,128)(2,1)} %copy.33), calls=%async_computation.1 | async-start | bytes 3670016 | tf_op jit(solution)/shard_map/all_to_all | solution.py:63
  180.9 1.7 fusion.11
  182.6 86.7 %all-to-all-done = bf16[28,224,128]{2,0,1:T(8,128)(2,1)} async-done(((bf16[28,224,128]{2,0,1:T(8,128)(2,1)}), bf16[28,224,128]{2,0,1:T(8,128)(2,1)}, u32[]{:S(2)}, u32[]{:S(2)}) %all-to-all-start) | async-done | bytes 1605664 | tf_op jit(solution)/shard_map/all_to_all | solution.py:63
  269.3 3.3 %copy.35 = bf16[8,28,28,128]{3,1,0,2:T(8,128)(2,1)} copy(bf16[8,28,28,128]{3,1,2,0:T(8,128)(2,1)} %bitcast.25) | data formatting | bytes 3211264 | tf_op jit(solution)/shard_map/all_to_all | solution.py:63
  272.6 2.4 all_to_all.16
  275.0 3.7 %copy.37 = bf16[224,28,128]{0,1,2:T(8,128)(2,1)} copy(bf16[224,28,128]{2,0,1:T(8,128)(2,1)S(1)} %all_to_all.16) | data formatting | bytes 3211264 | tf_op jit(solution)/shard_map/all_to_all | solution.py:63
  278.7 10.1 %copy.36 = bf16[224,112,128]{1,0,2:T(8,128)(2,1)} copy(bf16[224,112,128]{2,1,0:T(8,128)(2,1)} %all-gather.6.cloned.1.call-done) | data formatting | bytes 12845056 | tf_op jit(solution)/shard_map/all_gather | solution.py:42
  288.9 6.2 %bitcast_reduce_fusion = (f32[28,112]{1,0:T(8,128)S(1)}, f32[128,112,28]{1,2,0:T(8,128)S(1)}) fusion(bf16[224,112,128]{1,0,2:T(8,128)(2,1)} %copy.36, bf16[224,28,128]{0,1,2:T(8,128)(2,1)} %copy.37), kind=kOutput, calls=%fused_computation.45 | convolution fusion | flops 180229056 | bytes 9646336 | tf_op jit(solution)/shard_map/kic,kjc->ijc/dot_general | solution.py:39
  295.1 0.3 multiply_reduce_fusion
  295.5 0.3 multiply_convert_fusion
  295.8 1.7 copy.38
  297.5 2.3 fusion.74
  299.8 0.0 copy-start.4
  299.8 0.0 copy-start.7
  299.9 0.9 multiply_reduce_fusion.1
  300.8 0.0 copy-done.4
  300.8 0.0 copy-done.7
  300.8 3.7 %fusion.35 = f32[3136,512]{1,0:T(8,128)} fusion(f32[3136,128]{1,0:T(8,128)S(1)} %get-tuple-element.14, f32[128]{0:T(128)S(1)} %copy-done.7, f32[3136]{0:T(1024)S(1)} %add_rsqrt_fusion, f32[3136]{0:T(1024)S(1)} %broadcast_multiply_fusion, bf16[2,128,512]{2,1,0:T(8,128)(2,1)S(1)} %copy-done.4), kind=kOutput, calls=%fused_computation.63 | convolution fusion | flops 412647424 | bytes 8192512 | tf_op jit(solution)/shard_map/dot_general | solution.py:15
  304.5 0.0 copy-done
  304.5 6.3 %fusion.29 = bf16[3136,128]{1,0:T(8,128)(2,1)} fusion(f32[3136,128]{1,0:T(8,128)S(1)} %get-tuple-element.14, bf16[512,128]{1,0:T(8,128)(2,1)S(1)} %copy-done, f32[3136,512]{1,0:T(8,128)} %fusion.35, f32[128]{0:T(128)S(1)} %copy-done.7, f32[3136]{0:T(1024)S(1)} %add_rsqrt_fusion, f32[3136]{0:T(1024)S(1)} %broadcast_multiply_fusion, ...), kind=kOutput, calls=%fused_computation.43 | convolution fusion | flops 834125824 | bytes 10732032 | tf_op jit(solution)/shard_map/dot_general | solution.py:15
  (13 shorter events, 0.1 us)
Async XLA Ops:
  6.5 298.0 %copy-start = (bf16[512,128]{1,0:T(8,128)(2,1)S(1)}, bf16[512,128]{1,0:T(8,128)(2,1)}, u32[]{:S(2)}) copy-start(bf16[512,128]{1,0:T(8,128)(2,1)} %param.13) | copy-start | bytes 393220
  6.5 4.5 %copy-start.1 = (bf16[28,112,128]{2,1,0:T(8,128)(2,1)S(1)}, bf16[28,112,128]{2,1,0:T(8,128)(2,1)}, u32[]{:S(2)}) copy-start(bf16[28,112,128]{2,1,0:T(8,128)(2,1)} %param.7) | copy-start | bytes 2408452
  6.5 76.1 %all-gather.4.cloned.1.call-start = ((), (), s32[]{:S(2)}) async-start(), calls=%async_computation.2 | async-start | bytes 7225344 | tf_op jit(solution)/shard_map/all_gather | solution.py:50
  7.4 4.7 %copy-start.6 = (bf16[2,5,128,128]{3,2,1,0:T(8,128)(2,1)S(1)}, bf16[2,5,128,128]{3,2,1,0:T(8,128)(2,1)}, u32[]{:S(2)}) copy-start(bf16[2,5,128,128]{3,2,1,0:T(8,128)(2,1)} %param.9) | copy-start | bytes 983044
  13.9 120.5 %reduce-scatter.2.cloned.1.call-start = ((), (), s32[]{:S(2)}) async-start(), calls=%async_computation.3 | async-start | bytes 2752512 | tf_op jit(solution)/shard_map/reduce_scatter | solution.py:51
  106.7 66.2 %all-gather.8.cloned.1.call-start = ((), (), s32[]{:S(2)}) async-start(), calls=%async_computation.5 | async-start | bytes 2408448 | tf_op jit(solution)/shard_map/all_gather | solution.py:62
  134.5 4.2 %copy-start.2 = (bf16[112,28,128]{2,1,0:T(8,128)(2,1)S(1)}, bf16[112,28,128]{2,1,0:T(8,128)(2,1)}, u32[]{:S(2)}) copy-start(bf16[112,28,128]{2,1,0:T(8,128)(2,1)} %reduce-scatter.2.cloned.1.call-done) | copy-start | bytes 2408452
  136.3 3.7 %copy-start.3 = (f32[3136,128]{1,0:T(8,128)S(1)}, f32[3136,128]{1,0:T(8,128)}, u32[]{:S(2)}) copy-start(f32[3136,128]{1,0:T(8,128)} %fusion.20) | copy-start | bytes 4816900
  136.3 3.7 %copy-start.5 = (bf16[2,128,128]{2,1,0:T(8,128)(2,1)S(1)}, bf16[2,128,128]{2,1,0:T(8,128)(2,1)}, u32[]{:S(2)}) copy-start(bf16[2,128,128]{2,1,0:T(8,128)(2,1)} %param.10) | copy-start | bytes 196612
  145.2 133.5 %all-gather.6.cloned.1.call-start = ((), (), s32[]{:S(2)}) async-start(), calls=%async_computation.4 | async-start | bytes 7225344 | tf_op jit(solution)/shard_map/all_gather | solution.py:42
  176.3 93.0 %all-to-all-start = ((bf16[28,224,128]{2,0,1:T(8,128)(2,1)}), bf16[28,224,128]{2,0,1:T(8,128)(2,1)}, u32[]{:S(2)}, u32[]{:S(2)}) async-start(bf16[28,224,128]{2,0,1:T(8,128)(2,1)} %copy.33), calls=%async_computation.1 | async-start | bytes 3670016 | tf_op jit(solution)/shard_map/all_to_all | solution.py:63
  299.8 1.0 copy-start.4
  299.8 1.0 copy-start.7
Sparse Core Ops, SparseCore 0:
  14.1 68.5 all-gather.3
  106.9 27.5 reduce-scatter.1
  145.4 27.5 all-gather.7
  174.6 102.9 all-gather.5
where the time goes:
time: 318 us; the launch traced here: 317 us
  waiting for transfers between devices  204 us (64%)
  local copies, waits for them, and re-layouts  42.6 us (13%)
  matrix products  38.1 us (12%)
  other arithmetic  14.4 us (5%)
  between operations  13.4 us (4%)
  starting transfers between devices  4.91 us (2%)
    all_to_all x1, waiting for transfers between devices, on_device(): lax.all_to_all(panel_left, 'row', split_axis=1, concat_axis=0, tiled=True)  86.7 us
    all_gather x1, waiting for transfers between devices, on_device(): right_every = lax.all_gather(right, 'row', axis=0, tiled=True)  65.5 us
    all_gather x1, waiting for transfers between devices, on_device(): panel_left = lax.all_gather(left, 'col', axis=1, tiled=True)  25.9 us
    reduce_scatter x1, waiting for transfers between devices, on_device(): lax.psum_scatter(jnp.einsum('jkc,ikc->jic', right_every, left, preferred_...  25.8 us
    dot_general x14, matrix products, project(): return jnp.dot(flat, weight, preferred_element_type=jnp.float32)  22.8 us
    all_gather x1, local copies, waits for them, and re-layouts, incoming_fold(): lax.all_gather(right, 'row', axis=0, tiled=True)  10.1 us
    all_gather x1, local copies, waits for them, and re-layouts, on_device(): right_every = lax.all_gather(right, 'row', axis=0, tiled=True)  10.1 us
    all_to_all x3, local copies, waits for them, and re-layouts, on_device(): lax.all_to_all(panel_left, 'row', split_axis=1, concat_axis=0, tiled=True)  9.41 us
  transfers between devices with their start and end apart: 5, of which 4 were waited for; matrix products, arithmetic and copies ran while one was open for 6% of the time, Pallas kernels for 0%

commit v1 on v0

v1 whole, which is shorter than its diff:
```python
import functools

import jax
import jax.numpy as jnp
from jax import lax
from jax.experimental import pallas as pl
from jax.experimental.pallas import tpu as pltpu
from jax.sharding import PartitionSpec as P

GROUP = ("row", "col")


def normalize(values, gain):
    mean = jnp.mean(values, axis=-1, keepdims=True)
    centered = values - mean
    variance = jnp.mean(centered * centered, axis=-1, keepdims=True)
    return centered * lax.rsqrt(variance + 1e-05) * gain


def project(flat, weight):
    return jnp.dot(flat, weight, preferred_element_type=jnp.float32)


def exchange_kernel(n_row, n_col, x_ref, o_ref, send_sem, recv_sem, local_sem):
    n = n_row * n_col
    me = lax.axis_index("row") * n_col + lax.axis_index("col")

    def place(d):
        peer = lax.rem(me + d, n)
        return peer, {"row": peer // n_col, "col": lax.rem(peer, n_col)}

    barrier = pltpu.get_barrier_semaphore()

    def greet(d, _):
        pl.semaphore_signal(barrier, inc=1, device_id=place(d)[1], device_id_type=pl.DeviceIdType.MESH)
        return 0

    lax.fori_loop(1, n, greet, 0)
    own = pltpu.make_async_copy(x_ref.at[me], o_ref.at[me], local_sem)
    own.start()
    pl.semaphore_wait(barrier, n - 1)

    def send(d, _):
        peer, where = place(d)
        pltpu.make_async_remote_copy(
            src_ref=x_ref.at[peer], dst_ref=o_ref.at[me],
            send_sem=send_sem.at[d], recv_sem=recv_sem.at[d],
            device_id=where, device_id_type=pl.DeviceIdType.MESH,
        ).start()
        return 0

    lax.fori_loop(1, n, send, 0)

    def finish(d, _):
        peer, where = place(d)
        source = lax.rem(me - d + n, n)
        copy = pltpu.make_async_remote_copy(
            src_ref=x_ref.at[peer], dst_ref=o_ref.at[source],
            send_sem=send_sem.at[d], recv_sem=recv_sem.at[d],
            device_id=where, device_id_type=pl.DeviceIdType.MESH,
        )
        copy.wait_send()
        copy.wait_recv()
        return 0

    lax.fori_loop(1, n, finish, 0)
    own.wait()


def exchange(x, n_row, n_col, cid):
    n = n_row * n_col
    return pl.pallas_call(
        functools.partial(exchange_kernel, n_row, n_col),
        out_shape=jax.ShapeDtypeStruct(x.shape, x.dtype),
        in_specs=[pl.BlockSpec(memory_space=pltpu.VMEM)],
        out_specs=pl.BlockSpec(memory_space=pltpu.VMEM),
        scratch_shapes=[
            pltpu.SemaphoreType.DMA((n,)),
            pltpu.SemaphoreType.DMA((n,)),
            pltpu.SemaphoreType.DMA,
        ],
        compiler_params=pltpu.CompilerParams(
            collective_id=cid, has_side_effects=True, vmem_limit_bytes=40 * 1024 * 1024
        ),
        name=f"exchange_{cid}",
    )(x)


def pad_rows(x):
    short = -x.shape[1] % 16
    return jnp.pad(x, ((0, 0), (0, short), (0, 0))) if short else x


def on_device(n_row, n_col, pair, tri_gains, tri_proj, tri_out, trans_gain, trans_up, trans_down):
    rows, cols, width = pair.shape
    n = n_row * n_col
    cells = rows * cols
    each = width // n

    def update(pair, gains, weights, out_weight, spec, cid):
        flat = normalize(pair.reshape(-1, width).astype(jnp.float32), gains[0]).astype(jnp.bfloat16)

        def turned(weight):
            return lax.dot_general(weight, flat, (((0,), (1,)), ((), ())), preferred_element_type=jnp.float32)

        left = (jax.nn.sigmoid(turned(weights[1])) * turned(weights[0])).astype(jnp.bfloat16)
        right = (jax.nn.sigmoid(turned(weights[3])) * turned(weights[2])).astype(jnp.bfloat16)
        gate = jax.nn.sigmoid(project(flat, weights[4]))
        both = jnp.concatenate([left.reshape(n, each, cells), right.reshape(n, each, cells)], axis=1)
        both = exchange(pad_rows(both), n_row, n_col, cid)[:, : 2 * each]
        both = both.reshape(n_row, n_col, 2, each, rows, cols)
        both = jnp.transpose(both, (2, 3, 0, 4, 1, 5)).reshape(2, each, n_row * rows, n_col * cols)
        summed = jnp.einsum(spec, both[0], both[1], preferred_element_type=jnp.float32).astype(jnp.bfloat16)
        summed = summed.reshape(each, n_row, rows, n_col, cols)
        summed = jnp.transpose(summed, (1, 3, 0, 2, 4)).reshape(n, 2 * each, cells // 2)
        summed = exchange(pad_rows(summed), n_row, n_col, cid + 1)[:, : 2 * each]
        summed = jnp.transpose(summed.reshape(width, cells), (1, 0)).astype(jnp.float32)
        done = normalize(summed, gains[1]).astype(jnp.bfloat16)
        result = pair.reshape(-1, width).astype(jnp.float32) + gate * project(done, out_weight)
        return result.astype(jnp.bfloat16).reshape(pair.shape)

    pair_mid = update(pair, tri_gains[0], tri_proj[0], tri_out[0], "cik,cjk->cij", 0)
    pair_new = update(pair_mid, tri_gains[1], tri_proj[1], tri_out[1], "cki,ckj->cij", 2)
    flat = normalize(pair_new.reshape(-1, width).astype(jnp.float32), trans_gain).astype(jnp.bfloat16)
    inner = (jax.nn.silu(project(flat, trans_up[0])) * project(flat, trans_up[1])).astype(jnp.bfloat16)
    result = pair_new.reshape(-1, width).astype(jnp.float32) + project(inner, trans_down)
    return result.astype(jnp.bfloat16).reshape(rows, cols, width)


def solution(mesh):
    placed = (P(("rep", "row"), "col", None), P(), P(), P(), P(), P(), P())
    return jax.shard_map(
        functools.partial(on_device, mesh.shape["row"], mesh.shape["col"]),
        mesh=mesh,
        in_specs=placed,
        out_specs=P(("rep", "row"), "col", None),
        check_vma=False,
    )
```

time: 318 us -> 208 us (0.65)
  the two profiles are of different devices: /device:TPU:0 before, /device:TPU:11 now
where the time goes in v1:
time: 208 us; the launch traced here: 207 us
  Pallas kernels  127 us (61%)
  local copies, waits for them, and re-layouts  40.5 us (19%)
  matrix products  30.6 us (15%)
  other arithmetic  9.1 us (4%)
    pallas_call x4, Pallas kernels, exchange(): pl.pallas_call(functools.partial(exchange_kernel, n_row, n_col), out_shap...  127 us
    dot_general x6, matrix products, project(): return jnp.dot(flat, weight, preferred_element_type=jnp.float32)  17.8 us
    dot_general x8, matrix products, turned(): lax.dot_general(weight, flat, (((0,), (1,)), ((), ())), preferred_element...  10.6 us
    reshape x2, local copies, waits for them, and re-layouts, update(): both = both.reshape(n_row, n_col, 2, each, rows, cols)  9.15 us
    slice x4, local copies, waits for them, and re-layouts, update(): both[1]  6.76 us
    squeeze x2, local copies, waits for them, and re-layouts, update(): both[1]  4.46 us
    reduce_sum x5, other arithmetic, normalize(): variance = jnp.mean(centered * centered, axis=-1, keepdims=True)  4.38 us

profile of v1, /device:TPU:11, one launch (start us, length us, event | category | flops | bytes accessed | tf_op | source)
XLA Modules:
  0.0 207.3 jit_solution(7502941837340447830)
XLA Ops:
  0.0 1.3 slice_bitcast_fusion
  1.3 1.5 convert_reduce_fusion
  2.8 2.1 %multiply_reduce_fusion.4 = f32[28,112]{1,0:T(8,128)S(1)} fusion(bf16[28,112,128]{2,1,0:T(8,128)(2,1)} %param.7, f32[28,112]{1,0:T(8,128)S(1)} %broadcast_multiply_fusion.4), kind=kLoop, calls=%fused_computation.59 | loop fusion | flops 1602496 | bytes 827904 | tf_op jit(solution)/shard_map/reduce_sum | solution.py:16
  5.0 1.0 multiply_convert_fusion.4
  6.0 1.3 fusion.14
  7.3 1.1 fusion.32
  8.5 1.1 copy.19
  9.6 1.3 fusion.17
  10.9 2.0 fusion.33
  12.9 1.5 copy.18
  14.5 0.1 pad_maximum_fusion.x_ref
  14.6 40.5 %exchange_0.1 = bf16[16,16,3136]{2,1,0:T(8,128)(2,1)S(1)} custom-call(bf16[16,16,3136]{2,1,0:T(8,128)(2,1)S(1)} %pad_maximum_fusion.x_ref), custom_call_target="tpu_custom_call" | custom-call | tf_op jit(solution)/shard_map/exchange_0/pallas_call | solution.py:72
  55.1 4.6 %reshape.235 = bf16[8,2,2,8,28,112]{5,4,3,2,1,0:T(8,128)(2,1)} reshape(bf16[16,16,3136]{2,1,0:T(8,128)(2,1)S(1)} %exchange_0.1) | data formatting | bytes 3211264 | tf_op jit(solution)/shard_map/reshape | solution.py:111
  59.7 2.0 fusion.79
  61.6 1.9 copy.21
  63.5 3.0 %squeeze.64 = bf16[8,224,224]{2,1,0:T(8,128)(2,1)} reshape(bf16[1,8,8,28,2,112]{5,4,3,2,1,0:T(2,128)(2,1)} %copy.21) | data formatting | bytes 1605632 | tf_op jit(solution)/shard_map/squeeze | solution.py:113
  66.5 2.5 %fusion.20 = f32[3136,128]{1,0:T(8,128)} fusion(bf16[3136,128]{1,0:T(8,128)(2,1)S(1)} %bitcast.101, bf16[2,5,128,128]{3,2,1,0:T(8,128)(2,1)} %param.9), kind=kOutput, calls=%fused_computation.34 | convolution fusion | flops 103964672 | bytes 2441216 | tf_op jit(solution)/shard_map/dot_general | solution.py:21
  69.0 0.9 copy.20
  70.0 1.5 squeeze.63
  71.4 1.6 convolution_convert_fusion.1
  73.1 1.4 reshape.236
  74.4 1.4 copy.33
  75.8 1.3 reshape.237.x_ref
  77.1 23.3 %exchange_1.1 = bf16[16,16,1568]{2,1,0:T(8,128)(2,1)S(1)} custom-call(bf16[16,16,1568]{2,1,0:T(8,128)(2,1)S(1)} %reshape.237.x_ref), custom_call_target="tpu_custom_call" | custom-call | tf_op jit(solution)/shard_map/exchange_1/pallas_call | solution.py:72
  100.5 0.5 reshape.245
  101.0 0.0 copy-start.10
  101.0 0.1 reduce_sum.92
  101.1 0.2 multiply_reduce_fusion.1
  101.3 0.5 copy-done.10
  101.8 0.7 copy-done.7
  102.5 0.8 fusion.80
  103.4 0.9 multiply_reduce_fusion.3
  104.3 1.7 multiply_convert_fusion.3
  106.1 1.3 fusion.5
  107.4 1.1 fusion.30
  108.5 1.1 copy.24
  109.6 1.3 fusion.8
  111.0 1.1 fusion.31
  112.1 1.1 copy.23
  113.2 0.1 pad_maximum_fusion.1.x_ref
  113.3 39.9 %exchange_2.1 = bf16[16,16,3136]{2,1,0:T(8,128)(2,1)S(1)} custom-call(bf16[16,16,3136]{2,1,0:T(8,128)(2,1)S(1)} %pad_maximum_fusion.1.x_ref), custom_call_target="tpu_custom_call" | custom-call | tf_op jit(solution)/shard_map/exchange_2/pallas_call | solution.py:72
  153.2 4.6 %reshape.240 = bf16[8,2,2,8,28,112]{5,4,3,2,1,0:T(8,128)(2,1)} reshape(bf16[16,16,3136]{2,1,0:T(8,128)(2,1)S(1)} %exchange_2.1) | data formatting | bytes 3211264 | tf_op jit(solution)/shard_map/reshape | solution.py:111
  157.8 2.0 fusion.78
  159.7 0.9 copy.26
  160.7 1.5 squeeze.72
  162.1 2.5 %fusion.11 = f32[3136,128]{1,0:T(8,128)} fusion(bf16[3136,128]{1,0:T(8,128)(2,1)S(1)} %multiply_convert_fusion.3, bf16[2,5,128,128]{3,2,1,0:T(8,128)(2,1)} %param.9), kind=kOutput, calls=%fused_computation.22 | convolution fusion | flops 103964672 | bytes 2441216 | tf_op jit(solution)/shard_map/dot_general | solution.py:21
  164.7 0.9 copy.25
  165.6 0.5 squeeze.71
  166.2 0.5 convolution_convert_fusion
  166.6 0.4 reshape.241
  167.1 0.2 copy.32
  167.3 1.3 reshape.242.x_ref
  168.6 23.0 %exchange_3.1 = bf16[16,16,1568]{2,1,0:T(8,128)(2,1)S(1)} custom-call(bf16[16,16,1568]{2,1,0:T(8,128)(2,1)S(1)} %reshape.242.x_ref), custom_call_target="tpu_custom_call" | custom-call | tf_op jit(solution)/shard_map/exchange_3/pallas_call | solution.py:72
  191.6 0.5 reshape.246
  192.2 0.1 reduce_sum.96
  192.3 0.2 multiply_reduce_fusion
  192.5 1.1 copy-done.2
  193.6 0.5 copy-done.8
  194.1 0.9 fusion.81
  195.0 0.0 copy-start.9
  195.0 0.9 multiply_reduce_fusion.2
  196.0 0.2 copy-done.3
  196.1 3.6 %fusion.40 = f32[3136,512]{1,0:T(8,128)} fusion(f32[3136,128]{1,0:T(8,128)S(1)} %get-tuple-element.16, f32[128]{0:T(128)S(1)} %copy-done.12, f32[3136]{0:T(1024)S(1)} %add_rsqrt_fusion, f32[3136]{0:T(1024)S(1)} %broadcast_multiply_fusion, bf16[2,128,512]{2,1,0:T(8,128)(2,1)S(1)} %copy-done.9), kind=kOutput, calls=%fused_computation.71 | convolution fusion | flops 412647424 | bytes 8192512 | tf_op jit(solution)/shard_map/dot_general | solution.py:21
  199.8 7.5 %fusion.29 = bf16[3136,128]{1,0:T(8,128)(2,1)} fusion(f32[3136,128]{1,0:T(8,128)} %copy-done.3, bf16[512,128]{1,0:T(8,128)(2,1)S(1)} %copy-done, f32[3136,512]{1,0:T(8,128)} %fusion.40, f32[128]{0:T(128)S(1)} %copy-done.12, f32[3136]{0:T(1024)S(1)} %add_rsqrt_fusion, f32[3136]{0:T(1024)S(1)} %broadcast_multiply_fusion, bf16[2,128,512]{2,1,0:T(8,128)(2,1)S(1)} %copy-done.9), kind=kOutput, calls=%fused_computation.43 | convolution fusion | flops 834125824 | bytes 10732032 | tf_op jit(solution)/shard_map/dot_general | solution.py:21
  (29 shorter events, 0.1 us)
Async XLA Ops:
  0.0 199.8 %copy-start = (bf16[512,128]{1,0:T(8,128)(2,1)S(1)}, bf16[512,128]{1,0:T(8,128)(2,1)}, u32[]{:S(2)}) copy-start(bf16[512,128]{1,0:T(8,128)(2,1)} %param.13) | copy-start | bytes 393220
  0.0 5.0 %copy-start.4 = (bf16[28,112,128]{2,1,0:T(8,128)(2,1)S(1)}, bf16[28,112,128]{2,1,0:T(8,128)(2,1)}, u32[]{:S(2)}) copy-start(bf16[28,112,128]{2,1,0:T(8,128)(2,1)} %param.7) | copy-start | bytes 2408452
  70.0 1.5 copy-start.5
  101.0 0.8 copy-start.10
  101.1 1.4 copy-start.7
  103.3 2.7 %copy-start.1 = (f32[3136,128]{1,0:T(8,128)}, f32[3136,128]{1,0:T(8,128)S(1)}, u32[]{:S(2)}) copy-start(f32[3136,128]{1,0:T(8,128)S(1)} %get-tuple-element.14) | copy-start | bytes 4816900
  164.6 1.5 copy-start.6
  192.1 1.4 copy-start.2
  192.1 1.4 copy-start.11
  192.2 1.8 copy-start.8
  195.0 1.2 copy-start.3
  195.0 1.2 copy-start.9
  195.0 1.1 copy-start.12

commit v2 on v1

--- a/solution.py
+++ b/solution.py
@@ -86,6 +86,280 @@
     )(x)
 
 
+NT = (((1,), (1,)), ((), ()))
+STEP = 896
+
+
+def fused_kernel(
+    n_row, n_col, rows, cols,
+    x_ref, gains_ref, proj_ref, out_w_ref, tgain_ref, up_ref, down_ref, o_ref,
+    turned, gate, mid, summed, lefts, rights, outs,
+    send_a, recv_a, send_b, recv_b, send_c, recv_c, send_d, recv_d,
+    ssem_a, rsem_a, ssem_b, rsem_b, ssem_c, rsem_c, ssem_d, rsem_d, local_sem,
+):
+    n = n_row * n_col
+    cells = rows * cols
+    each = 8
+    all_rows = n_row * rows
+    half = cells // 2
+    half_rows = rows // 2
+    back_tiles = recv_b.shape[2] // 128
+    row = lax.axis_index("row")
+    col = lax.axis_index("col")
+    me = row * n_col + col
+    f32, bf16 = jnp.float32, jnp.bfloat16
+    starts = list(range(0, cells, STEP))
+    padded = send_a.shape[2]
+    lane = lax.broadcasted_iota(jnp.int32, (8, 128), 1)
+
+    def place(d):
+        peer = lax.rem(me + d, n)
+        return peer, {"row": peer // n_col, "col": lax.rem(peer, n_col)}
+
+    barrier = pltpu.get_barrier_semaphore()
+
+    def greet(d, _):
+        pl.semaphore_signal(barrier, inc=1, device_id=place(d)[1], device_id_type=pl.DeviceIdType.MESH)
+        return 0
+
+    lax.fori_loop(1, n, greet, 0)
+
+    for u in range(2):
+        for m in range(4):
+            turned[u, m * 128 : (m + 1) * 128, :] = proj_ref[u, m].astype(f32).T.astype(bf16)
+    tail = cells - cells // 128 * 128
+    if tail:
+        zero = jnp.zeros((n, 16, 128), bf16)
+        send_a[:, :, padded - 128 :] = zero
+        send_c[:, :, padded - 128 :] = zero
+
+    def remote(send, recv, ssem, rsem, k, lo, size, d, source):
+        peer, where = place(d)
+        return pltpu.make_async_remote_copy(
+            src_ref=send.at[peer, :, pl.ds(lo, size)],
+            dst_ref=recv.at[source, :, pl.ds(lo, size)],
+            send_sem=ssem.at[k, d], recv_sem=rsem.at[k, d],
+            device_id=where, device_id_type=pl.DeviceIdType.MESH,
+        )
+
+    def span(k):
+        lo = starts[k]
+        return lo, (padded if k == len(starts) - 1 else lo + STEP) - lo
+
+    def prepare(u, values, lo, size, send):
+        flat = normalize(values, gains_ref[2 * u : 2 * u + 1, :]).astype(bf16)
+        gate[lo : lo + size, :] = jax.nn.sigmoid(project(flat, proj_ref[u, 4]))
+        for side in range(2):
+            value = lax.dot_general(
+                turned[u, 256 * side : 256 * side + 128, :], flat, NT, preferred_element_type=f32
+            )
+            scale = lax.dot_general(
+                turned[u, 256 * side + 128 : 256 * side + 256, :], flat, NT, preferred_element_type=f32
+            )
+            held = (jax.nn.sigmoid(scale) * value).astype(bf16)
+            send[:, each * side : each * side + each, lo : lo + size] = held.reshape(n, each, size)
+
+    def send_chunk(k, send, recv, ssem, rsem):
+        lo, size = span(k)
+
+        def one(d, _):
+            remote(send, recv, ssem, rsem, k, lo, size, d, me).start()
+            return 0
+
+        lax.fori_loop(1, n, one, 0)
+
+    def shifted(tiles, start):
+        t, s = start // 128, start % 128
+        if s == 0:
+            return tiles[t]
+        first = pltpu.roll(tiles[t], 128 - s, 1)
+        if s + cols <= 128:
+            return first
+        return jnp.where(lane < 128 - s, first, pltpu.roll(tiles[t + 1], 128 - s, 1))
+
+    def unpack(recv, source):
+        r, q = source // n_col, lax.rem(source, n_col)
+        base = q * (each * all_rows) + r * rows
+        tiles = [recv[source, :, 128 * t : 128 * t + 128].astype(f32) for t in range(padded // 128)]
+        for side, held in ((0, lefts), (1, rights)):
+            mine = [t[each * side : each * side + each] for t in tiles]
+            for i in range(rows):
+                value = jnp.where(lane < cols, shifted(mine, cols * i), 0.0)
+                held[pl.ds(base + i, each, stride=all_rows), :] = value
+
+    def receive(send, recv, ssem, rsem):
+        own = pltpu.make_async_copy(send.at[me], recv.at[me], local_sem)
+        own.start()
+        own.wait()
+        unpack(recv, me)
+
+        def one(d, _):
+            source = lax.rem(me - d + n, n)
+            for k in range(len(starts)):
+                lo, size = span(k)
+                remote(send, recv, ssem, rsem, k, lo, size, d, source).wait_recv()
+            unpack(recv, source)
+            return 0
+
+        lax.fori_loop(1, n, one, 0)
+
+    def channel(held, q, c, offset, size):
+        at = pl.multiple_of(q * (each * all_rows) + c * all_rows + offset, 8)
+        return held[pl.ds(at, size), :]
+
+    def outgoing(c, _):
+        left = [channel(lefts, q, c, 0, all_rows).astype(bf16) for q in range(n_col)]
+        for jq in range(n_col):
+            total = None
+            for q in range(n_col):
+                right = channel(rights, q, c, jq * cols, 128).astype(bf16)
+                term = lax.dot_general(left[q], right, NT, preferred_element_type=f32)
+                total = term if total is None else total + term
+            outs[pl.ds(jq * (each * all_rows) + c, all_rows, stride=each), :] = total
+        return 0
+
+    def incoming(c, _):
+        right = [channel(rights, q, c, 0, all_rows).astype(bf16) for q in range(n_col)]
+        for iq in range(n_col):
+            left = channel(lefts, iq, c, 0, all_rows).T.astype(bf16)
+            for jq in range(n_col):
+                total = project(left, right[jq])[:cols]
+                at = jq * (each * all_rows) + iq * cols * each + c
+                outs[pl.ds(at, cols, stride=each), :] = total
+        return 0
+
+    def pack(send, dest):
+        r, q = dest // n_col, lax.rem(dest, n_col)
+        base = q * (each * all_rows) + r * rows * each
+        for t in range(back_tiles):
+            parts = []
+            for h in range(2):
+                total = jnp.zeros((8, 128), f32)
+                for i in range(half_rows):
+                    at = i * cols - 128 * t
+                    if at >= 128 or at + cols <= 0:
+                        continue
+                    spot = pl.multiple_of(base + (h * half_rows + i) * each, 8)
+                    value = outs[pl.ds(spot, each), :]
+                    if at % 128:
+                        value = pltpu.roll(value, at % 128, 1)
+                    total = jnp.where((lane >= at) & (lane < at + cols), value, total)
+                parts.append(total)
+            send[dest, :, 128 * t : 128 * t + 128] = jnp.concatenate(parts, axis=0).astype(bf16)
+
+    def give_back(send, recv, ssem, rsem):
+        width = send.shape[2]
+
+        def one(d, _):
+            pack(send, place(d)[0])
+            remote(send, recv, ssem, rsem, 0, 0, width, d, me).start()
+            return 0
+
+        lax.fori_loop(1, n, one, 0)
+        pack(send, me)
+        own = pltpu.make_async_copy(send.at[me], recv.at[me], local_sem)
+        own.start()
+        own.wait()
+
+        def done(d, _):
+            remote(send, recv, ssem, rsem, 0, 0, width, d, lax.rem(me - d + n, n)).wait_recv()
+            return 0
+
+        lax.fori_loop(1, n, done, 0)
+        for t in range(back_tiles):
+            tile = recv[:, :, 128 * t : 128 * t + 128].astype(f32)
+            keep = min(128, half - 128 * t)
+            for h in range(2):
+                piece = tile[:, each * h : each * h + each, :].reshape(n * each, 128).T
+                summed[h * half + 128 * t : h * half + 128 * t + keep, :] = piece[:keep]
+
+    def finish(u, before, lo, size):
+        done = normalize(summed[pl.ds(lo, size), :], gains_ref[2 * u + 1 : 2 * u + 2, :]).astype(bf16)
+        result = before.astype(f32) + gate[pl.ds(lo, size), :] * project(done, out_w_ref[u])
+        return result.astype(bf16)
+
+    for k, lo in enumerate(starts):
+        size = min(STEP, cells - lo)
+        prepare(0, x_ref[lo : lo + size, :].astype(f32), lo, size, send_a)
+        if k == 0:
+            pl.semaphore_wait(barrier, n - 1)
+        send_chunk(k, send_a, recv_a, ssem_a, rsem_a)
+    receive(send_a, recv_a, ssem_a, rsem_a)
+    lax.fori_loop(0, each, outgoing, 0)
+    give_back(send_b, recv_b, ssem_b, rsem_b)
+    for k, lo in enumerate(starts):
+        size = min(STEP, cells - lo)
+        held = finish(0, x_ref[lo : lo + size, :], lo, size)
+        mid[lo : lo + size, :] = held
+        prepare(1, held.astype(f32), lo, size, send_c)
+        send_chunk(k, send_c, recv_c, ssem_c, rsem_c)
+    receive(send_c, recv_c, ssem_c, rsem_c)
+    lax.fori_loop(0, each, incoming, 0)
+    give_back(send_d, recv_d, ssem_d, rsem_d)
+
+    last = STEP // 2
+
+    def transition(k, _):
+        lo = pl.multiple_of(k * last, 16)
+        new = finish(1, mid[pl.ds(lo, last), :], lo, last).astype(f32)
+        flat = normalize(new, tgain_ref[...]).astype(bf16)
+        first = project(flat, up_ref[0])
+        inner = (first * jax.nn.sigmoid(first) * project(flat, up_ref[1])).astype(bf16)
+        o_ref[pl.ds(lo, last), :] = (new + project(inner, down_ref[...])).astype(bf16)
+        return 0
+
+    lax.fori_loop(0, cells // last, transition, 0)
+
+    def drain(d, _):
+        for send, recv, ssem, rsem in ((send_a, recv_a, ssem_a, rsem_a), (send_c, recv_c, ssem_c, rsem_c)):
+            for k in range(len(starts)):
+                lo, size = span(k)
+                remote(send, recv, ssem, rsem, k, lo, size, d, me).wait_send()
+        for send, recv, ssem, rsem in ((send_b, recv_b, ssem_b, rsem_b), (send_d, recv_d, ssem_d, rsem_d)):
+            remote(send, recv, ssem, rsem, 0, 0, send.shape[2], d, me).wait_send()
+        return 0
+
+    lax.fori_loop(1, n, drain, 0)
+
+
+def fused(n_row, n_col, pair, tri_gains, tri_proj, tri_out, trans_gain, trans_up, trans_down):
+    rows, cols, width = pair.shape
+    n = n_row * n_col
+    cells = rows * cols
+    up128 = lambda v: -(-v // 128) * 128
+    ahead = pltpu.VMEM((n, 16, up128(cells)), jnp.bfloat16)
+    back = pltpu.VMEM((n, 16, up128(cells // 2)), jnp.bfloat16)
+    chunks = -(-cells // STEP)
+    panel = pltpu.VMEM((n_col * 8 * n_row * rows + 16, 128), jnp.float32)
+    many = pltpu.SemaphoreType.DMA((chunks, n))
+    few = pltpu.SemaphoreType.DMA((1, n))
+    whole = pl.BlockSpec(memory_space=pltpu.VMEM)
+    out = pl.pallas_call(
+        functools.partial(fused_kernel, n_row, n_col, rows, cols),
+        out_shape=jax.ShapeDtypeStruct((cells, width), pair.dtype),
+        in_specs=[whole] * 7,
+        out_specs=whole,
+        scratch_shapes=[
+            pltpu.VMEM((2, 4 * width, width), jnp.bfloat16),
+            pltpu.VMEM((cells, width), jnp.float32),
+            pltpu.VMEM((cells, width), jnp.bfloat16),
+            pltpu.VMEM((cells, width), jnp.float32),
+            panel, panel, panel,
+            ahead, ahead, back, back, ahead, ahead, back, back,
+            many, many, few, few, many, many, few, few,
+            pltpu.SemaphoreType.DMA,
+        ],
+        compiler_params=pltpu.CompilerParams(
+            collective_id=4, has_side_effects=True, vmem_limit_bytes=56 * 1024 * 1024
+        ),
+        name="fused",
+    )(
+        pair.reshape(cells, width), tri_gains.reshape(4, width), tri_proj, tri_out,
+        trans_gain.reshape(1, width), trans_up, trans_down,
+    )
+    return out.reshape(rows, cols, width)
+
+
 def pad_rows(x):
     short = -x.shape[1] % 16
     return jnp.pad(x, ((0, 0), (0, short), (0, 0))) if short else x
@@ -96,6 +370,8 @@
     n = n_row * n_col
     cells = rows * cols
     each = width // n
+    if each == 8 and width == 128 and n_row * rows == n_col * cols and cols % 16 == 0 and cells % (STEP // 2) == 0:
+        return fused(n_row, n_col, pair, tri_gains, tri_proj, tri_out, trans_gain, trans_up, trans_down)
 
     def update(pair, gains, weights, out_weight, spec, cid):
         flat = normalize(pair.reshape(-1, width).astype(jnp.float32), gains[0]).astype(jnp.bfloat16)

time: 208 us -> 141 us (0.68)
  local copies, waits for them, and re-layouts: 40.5 us -> 2.08 us
  matrix products: 30.6 us -> 0 us
  Pallas kernels: 127 us -> 138 us
  other arithmetic: 9.1 us -> 0 us
    dot_general x16 -> x0, matrix products: 30.6 us -> none  [the longest x6 17.8 us: project(): return jnp.dot(flat, weight, preferred_element_type=jnp.float32)]
    reshape x8 -> x0, local copies, waits for them, and re-layouts: 15.2 us -> none  [the longest x2 9.15 us: update(): both = both.reshape(n_row, n_col, 2, each, rows, cols)]
    pallas_call x4 -> x1, Pallas kernels: 127 us -> 138 us  [fused(): pl.pallas_call(functools.partial(fused_kernel, n_row, n_col, rows, cols),...]
    slice x6 -> x0, local copies, waits for them, and re-layouts: 8.65 us -> none  [the longest x4 6.76 us: update(): both[1]]
    squeeze x4 -> x0, local copies, waits for them, and re-layouts: 6.46 us -> none  [the longest x2 4.46 us: update(): both[1]]
    reduce_sum x8 -> x0, other arithmetic: 6.01 us -> none  [the longest x5 4.38 us: normalize(): variance = jnp.mean(centered * centered, axis=-1, keepdims=True)]
    convert_element_type x6 -> x0, local copies, waits for them, and re-layouts: 5.85 us -> none  [the longest x2 2.64 us: update(): (jax.nn.sigmoid(turned(weights[1])) * turned(weights[0])).astype(jnp.bflo...]
    convert_element_type x2 -> x0, other arithmetic: 2.78 us -> none  [update(): normalize(pair.reshape(-1, width).astype(jnp.float32), gains[0])]
where the time goes in v2:
time: 141 us; the launch traced here: 140 us
  Pallas kernels  138 us (98%)
  local copies, waits for them, and re-layouts  2.08 us (1%)
    pallas_call x1, Pallas kernels, fused(): pl.pallas_call(functools.partial(fused_kernel, n_row, n_col, rows, cols),...  138 us

profile of v2, /device:TPU:11, one launch (start us, length us, event | category | flops | bytes accessed | tf_op | source)
XLA Modules:
  0.0 140.5 jit_solution(5820180487065200123)
XLA Ops:
  0.0 138.4 %fused.1 = bf16[3136,128]{1,0:T(8,128)(2,1)} custom-call(bf16[3136,128]{1,0:T(8,128)(2,1)} %bitcast.5, f32[4,128]{1,0:T(4,128)} %bitcast.6, bf16[2,5,128,128]{3,2,1,0:T(8,128)(2,1)} %proj_ref.1, bf16[2,128,128]{2,1,0:T(8,128)(2,1)} %out_w_ref.1, f32[1,128]{1,0:T(1,128)} %bitcast.7, bf16[2,128,512]{2,1,0:T(8,128)(2,1)} %up_ref.1, bf16[512,128]{1,0:T(8,128)(2,1)} %down_ref.1), custom_call_target="tpu_custom_call" | custom-call | tf_op jit(solution)/shard_map/fused/pallas_call | solution.py:337
  138.4 2.1 %copy.9 = bf16[28,112,128]{2,1,0:T(8,128)(2,1)} copy(bf16[28,112,128]{2,1,0:T(8,128)(2,1)} %bitcast.4) | data formatting | bytes 1605632

commit v3 on v2

--- a/solution.py
+++ b/solution.py
@@ -87,7 +87,7 @@
 
 
 NT = (((1,), (1,)), ((), ()))
-STEP = 896
+TALL = 8
 
 
 def fused_kernel(
@@ -95,34 +95,42 @@
     x_ref, gains_ref, proj_ref, out_w_ref, tgain_ref, up_ref, down_ref, o_ref,
     turned, gate, mid, summed, lefts, rights, outs,
     send_a, recv_a, send_b, recv_b, send_c, recv_c, send_d, recv_d,
-    ssem_a, rsem_a, ssem_b, rsem_b, ssem_c, rsem_c, ssem_d, rsem_d, local_sem,
+    ssem_a, rsem_a, ssem_b, rsem_b, ssem_c, rsem_c, ssem_d, rsem_d,
 ):
     n = n_row * n_col
     cells = rows * cols
     each = 8
     all_rows = n_row * rows
-    half = cells // 2
-    half_rows = rows // 2
-    back_tiles = recv_b.shape[2] // 128
+    step = TALL * cols
+    h = n // 2
     row = lax.axis_index("row")
     col = lax.axis_index("col")
     me = row * n_col + col
     f32, bf16 = jnp.float32, jnp.bfloat16
-    starts = list(range(0, cells, STEP))
+    starts = list(range(0, cells, step))
     padded = send_a.shape[2]
     lane = lax.broadcasted_iota(jnp.int32, (8, 128), 1)
 
-    def place(d):
-        peer = lax.rem(me + d, n)
-        return peer, {"row": peer // n_col, "col": lax.rem(peer, n_col)}
+    def place(s):
+        side = lax.rem(me // h + 1 + s // h, 2)
+        peer = side * h + lax.rem(lax.rem(me, h) + s, h)
+        source = side * h + lax.rem(lax.rem(me, h) + n - s, h)
+        return peer, source, {"row": peer // n_col, "col": lax.rem(peer, n_col)}
+
+    def peers(body):
+        def one(s, _):
+            body(s)
+            return 0
+
+        lax.fori_loop(0, h, one, 0)
+        lax.fori_loop(h + 1, n, one, 0)
 
     barrier = pltpu.get_barrier_semaphore()
 
-    def greet(d, _):
-        pl.semaphore_signal(barrier, inc=1, device_id=place(d)[1], device_id_type=pl.DeviceIdType.MESH)
-        return 0
-
-    lax.fori_loop(1, n, greet, 0)
+    def greet(s):
+        pl.semaphore_signal(barrier, inc=1, device_id=place(s)[2], device_id_type=pl.DeviceIdType.MESH)
+
+    peers(greet)
 
     for u in range(2):
         for m in range(4):
@@ -133,18 +141,18 @@
         send_a[:, :, padded - 128 :] = zero
         send_c[:, :, padded - 128 :] = zero
 
-    def remote(send, recv, ssem, rsem, k, lo, size, d, source):
-        peer, where = place(d)
+    def remote(send, recv, ssem, rsem, k, lo, size, s, arriving):
+        peer, source, where = place(s)
         return pltpu.make_async_remote_copy(
             src_ref=send.at[peer, :, pl.ds(lo, size)],
-            dst_ref=recv.at[source, :, pl.ds(lo, size)],
-            send_sem=ssem.at[k, d], recv_sem=rsem.at[k, d],
+            dst_ref=recv.at[source if arriving else me, :, pl.ds(lo, size)],
+            send_sem=ssem.at[k, s], recv_sem=rsem.at[k, s],
             device_id=where, device_id_type=pl.DeviceIdType.MESH,
         )
 
     def span(k):
         lo = starts[k]
-        return lo, (padded if k == len(starts) - 1 else lo + STEP) - lo
+        return lo, (padded if k == len(starts) - 1 else lo + step) - lo
 
     def prepare(u, values, lo, size, send):
         flat = normalize(values, gains_ref[2 * u : 2 * u + 1, :]).astype(bf16)
@@ -161,12 +169,8 @@
 
     def send_chunk(k, send, recv, ssem, rsem):
         lo, size = span(k)
-
-        def one(d, _):
-            remote(send, recv, ssem, rsem, k, lo, size, d, me).start()
-            return 0
-
-        lax.fori_loop(1, n, one, 0)
+        peers(lambda s: remote(send, recv, ssem, rsem, k, lo, size, s, False).start())
+        unpack(send, me, k)
 
     def shifted(tiles, start):
         t, s = start // 128, start % 128
@@ -177,31 +181,26 @@
             return first
         return jnp.where(lane < 128 - s, first, pltpu.roll(tiles[t + 1], 128 - s, 1))
 
-    def unpack(recv, source):
+    def unpack(ref, source, k):
+        lo, size = span(k)
         r, q = source // n_col, lax.rem(source, n_col)
         base = q * (each * all_rows) + r * rows
-        tiles = [recv[source, :, 128 * t : 128 * t + 128].astype(f32) for t in range(padded // 128)]
+        tiles = [ref[source, :, lo + at : lo + at + 128].astype(f32) for at in range(0, size, 128)]
         for side, held in ((0, lefts), (1, rights)):
             mine = [t[each * side : each * side + each] for t in tiles]
-            for i in range(rows):
+            for i in range(min(TALL, rows - TALL * k)):
                 value = jnp.where(lane < cols, shifted(mine, cols * i), 0.0)
-                held[pl.ds(base + i, each, stride=all_rows), :] = value
-
-    def receive(send, recv, ssem, rsem):
-        own = pltpu.make_async_copy(send.at[me], recv.at[me], local_sem)
-        own.start()
-        own.wait()
-        unpack(recv, me)
-
-        def one(d, _):
-            source = lax.rem(me - d + n, n)
-            for k in range(len(starts)):
-                lo, size = span(k)
-                remote(send, recv, ssem, rsem, k, lo, size, d, source).wait_recv()
-            unpack(recv, source)
-            return 0
-
-        lax.fori_loop(1, n, one, 0)
+                held[pl.ds(base + TALL * k + i, each, stride=all_rows), :] = value
+
+    def receive(order, send, recv, ssem, rsem):
+        for k in order:
+            lo, size = span(k)
+
+            def one(s):
+                remote(send, recv, ssem, rsem, k, lo, size, s, True).wait_recv()
+                unpack(recv, place(s)[1], k)
+
+            peers(one)
 
     def channel(held, q, c, offset, size):
         at = pl.multiple_of(q * (each * all_rows) + c * all_rows + offset, 8)
@@ -228,76 +227,83 @@
                 outs[pl.ds(at, cols, stride=each), :] = total
         return 0
 
-    def pack(send, dest):
+    def pack(ref, dest, g):
         r, q = dest // n_col, lax.rem(dest, n_col)
         base = q * (each * all_rows) + r * rows * each
-        for t in range(back_tiles):
+        for t in range(step // 128):
             parts = []
-            for h in range(2):
+            for k in (g, g + 2):
                 total = jnp.zeros((8, 128), f32)
-                for i in range(half_rows):
+                for i in range(min(TALL, rows - TALL * k)):
                     at = i * cols - 128 * t
                     if at >= 128 or at + cols <= 0:
                         continue
-                    spot = pl.multiple_of(base + (h * half_rows + i) * each, 8)
+                    spot = pl.multiple_of(base + (TALL * k + i) * each, 8)
                     value = outs[pl.ds(spot, each), :]
                     if at % 128:
                         value = pltpu.roll(value, at % 128, 1)
                     total = jnp.where((lane >= at) & (lane < at + cols), value, total)
                 parts.append(total)
-            send[dest, :, 128 * t : 128 * t + 128] = jnp.concatenate(parts, axis=0).astype(bf16)
+            lo = g * step + 128 * t
+            ref[dest, :, lo : lo + 128] = jnp.concatenate(parts, axis=0).astype(bf16)
 
     def give_back(send, recv, ssem, rsem):
-        width = send.shape[2]
-
-        def one(d, _):
-            pack(send, place(d)[0])
-            remote(send, recv, ssem, rsem, 0, 0, width, d, me).start()
-            return 0
-
-        lax.fori_loop(1, n, one, 0)
-        pack(send, me)
-        own = pltpu.make_async_copy(send.at[me], recv.at[me], local_sem)
-        own.start()
-        own.wait()
-
-        def done(d, _):
-            remote(send, recv, ssem, rsem, 0, 0, width, d, lax.rem(me - d + n, n)).wait_recv()
-            return 0
-
-        lax.fori_loop(1, n, done, 0)
-        for t in range(back_tiles):
-            tile = recv[:, :, 128 * t : 128 * t + 128].astype(f32)
-            keep = min(128, half - 128 * t)
-            for h in range(2):
-                piece = tile[:, each * h : each * h + each, :].reshape(n * each, 128).T
-                summed[h * half + 128 * t : h * half + 128 * t + keep, :] = piece[:keep]
+        for g in range(2):
+
+            def one(s):
+                pack(send, place(s)[0], g)
+                remote(send, recv, ssem, rsem, g, g * step, step, s, False).start()
+
+            peers(one)
+        for g in range(2):
+            pack(recv, me, g)
+
+    def take_back(g, send, recv, ssem, rsem):
+        peers(lambda s: remote(send, recv, ssem, rsem, g, g * step, step, s, True).wait_recv())
+        for t in range(step // 128):
+            lo = g * step + 128 * t
+            tile = recv[:, :, lo : lo + 128].astype(f32)
+            for half in range(2):
+                at = (g + 2 * half) * step + 128 * t
+                keep = min(128, cells - at)
+                if keep > 0:
+                    piece = tile[:, each * half : each * half + each, :].reshape(n * each, 128).T
+                    summed[at : at + keep, :] = piece[:keep]
 
     def finish(u, before, lo, size):
         done = normalize(summed[pl.ds(lo, size), :], gains_ref[2 * u + 1 : 2 * u + 2, :]).astype(bf16)
         result = before.astype(f32) + gate[pl.ds(lo, size), :] * project(done, out_w_ref[u])
         return result.astype(bf16)
 
-    for k, lo in enumerate(starts):
-        size = min(STEP, cells - lo)
+    def bounds(k):
+        return starts[k], min(step, cells - starts[k])
+
+    ahead_a = (send_a, recv_a, ssem_a, rsem_a)
+    back_a = (send_b, recv_b, ssem_b, rsem_b)
+    ahead_b = (send_c, recv_c, ssem_c, rsem_c)
+    back_b = (send_d, recv_d, ssem_d, rsem_d)
+    for k in range(4):
+        lo, size = bounds(k)
         prepare(0, x_ref[lo : lo + size, :].astype(f32), lo, size, send_a)
         if k == 0:
             pl.semaphore_wait(barrier, n - 1)
-        send_chunk(k, send_a, recv_a, ssem_a, rsem_a)
-    receive(send_a, recv_a, ssem_a, rsem_a)
+        send_chunk(k, *ahead_a)
+    receive((0, 1, 2, 3), *ahead_a)
     lax.fori_loop(0, each, outgoing, 0)
-    give_back(send_b, recv_b, ssem_b, rsem_b)
-    for k, lo in enumerate(starts):
-        size = min(STEP, cells - lo)
-        held = finish(0, x_ref[lo : lo + size, :], lo, size)
-        mid[lo : lo + size, :] = held
-        prepare(1, held.astype(f32), lo, size, send_c)
-        send_chunk(k, send_c, recv_c, ssem_c, rsem_c)
-    receive(send_c, recv_c, ssem_c, rsem_c)
+    give_back(*back_a)
+    for g in range(2):
+        take_back(g, *back_a)
+        for k in (g, g + 2):
+            lo, size = bounds(k)
+            held = finish(0, x_ref[lo : lo + size, :], lo, size)
+            mid[lo : lo + size, :] = held
+            prepare(1, held.astype(f32), lo, size, send_c)
+            send_chunk(k, *ahead_b)
+    receive((0, 2, 1, 3), *ahead_b)
     lax.fori_loop(0, each, incoming, 0)
-    give_back(send_d, recv_d, ssem_d, rsem_d)
-
-    last = STEP // 2
+    give_back(*back_b)
+
+    last = step // 2
 
     def transition(k, _):
         lo = pl.multiple_of(k * last, 16)
@@ -308,18 +314,22 @@
         o_ref[pl.ds(lo, last), :] = (new + project(inner, down_ref[...])).astype(bf16)
         return 0
 
-    lax.fori_loop(0, cells // last, transition, 0)
-
-    def drain(d, _):
-        for send, recv, ssem, rsem in ((send_a, recv_a, ssem_a, rsem_a), (send_c, recv_c, ssem_c, rsem_c)):
-            for k in range(len(starts)):
+    for g in range(2):
+        take_back(g, *back_b)
+        for k in (g, g + 2):
+            lo, size = bounds(k)
+            lax.fori_loop(lo // last, (lo + size) // last, transition, 0)
+
+    def drain(s):
+        for held in (ahead_a, ahead_b):
+            for k in range(4):
                 lo, size = span(k)
-                remote(send, recv, ssem, rsem, k, lo, size, d, me).wait_send()
-        for send, recv, ssem, rsem in ((send_b, recv_b, ssem_b, rsem_b), (send_d, recv_d, ssem_d, rsem_d)):
-            remote(send, recv, ssem, rsem, 0, 0, send.shape[2], d, me).wait_send()
-        return 0
-
-    lax.fori_loop(1, n, drain, 0)
+                remote(*held, k, lo, size, s, True).wait_send()
+        for held in (back_a, back_b):
+            for g in range(2):
+                remote(*held, g, g * step, step, s, True).wait_send()
+
+    peers(drain)
 
 
 def fused(n_row, n_col, pair, tri_gains, tri_proj, tri_out, trans_gain, trans_up, trans_down):
@@ -328,11 +338,10 @@
     cells = rows * cols
     up128 = lambda v: -(-v // 128) * 128
     ahead = pltpu.VMEM((n, 16, up128(cells)), jnp.bfloat16)
-    back = pltpu.VMEM((n, 16, up128(cells // 2)), jnp.bfloat16)
-    chunks = -(-cells // STEP)
+    back = pltpu.VMEM((n, 16, 2 * TALL * cols), jnp.bfloat16)
     panel = pltpu.VMEM((n_col * 8 * n_row * rows + 16, 128), jnp.float32)
-    many = pltpu.SemaphoreType.DMA((chunks, n))
-    few = pltpu.SemaphoreType.DMA((1, n))
+    many = pltpu.SemaphoreType.DMA((4, n))
+    few = pltpu.SemaphoreType.DMA((2, n))
     whole = pl.BlockSpec(memory_space=pltpu.VMEM)
     out = pl.pallas_call(
         functools.partial(fused_kernel, n_row, n_col, rows, cols),
@@ -347,7 +356,6 @@
             panel, panel, panel,
             ahead, ahead, back, back, ahead, ahead, back, back,
             many, many, few, few, many, many, few, few,
-            pltpu.SemaphoreType.DMA,
         ],
         compiler_params=pltpu.CompilerParams(
             collective_id=4, has_side_effects=True, vmem_limit_bytes=56 * 1024 * 1024
@@ -370,7 +378,8 @@
     n = n_row * n_col
     cells = rows * cols
     each = width // n
-    if each == 8 and width == 128 and n_row * rows == n_col * cols and cols % 16 == 0 and cells % (STEP // 2) == 0:
+    square = n_row * rows == n_col * cols
+    if each == 8 and width == 128 and square and n % 2 == 0 and cols % 16 == 0 and rows in (28, 32):
         return fused(n_row, n_col, pair, tri_gains, tri_proj, tri_out, trans_gain, trans_up, trans_down)
 
     def update(pair, gains, weights, out_weight, spec, cid):

time: 141 us -> 139 us (0.986)
  the two profiles are of different devices: /device:TPU:11 before, /device:TPU:0 now
where the time goes in v3:
time: 139 us
  Pallas kernels  137 us (99%)
  local copies, waits for them, and re-layouts  2.08 us (1%)
    pallas_call x1, Pallas kernels, fused(): pl.pallas_call(functools.partial(fused_kernel, n_row, n_col, rows, cols),...  137 us

profile of v3, /device:TPU:0, one launch (start us, length us, event | category | flops | bytes accessed | tf_op | source)
XLA Modules:
  0.0 138.7 jit_solution(4562292693661118805)
XLA Ops:
  0.0 136.6 %fused.1 = bf16[3136,128]{1,0:T(8,128)(2,1)} custom-call(bf16[3136,128]{1,0:T(8,128)(2,1)} %bitcast.5, f32[4,128]{1,0:T(4,128)} %bitcast.6, bf16[2,5,128,128]{3,2,1,0:T(8,128)(2,1)} %proj_ref.1, bf16[2,128,128]{2,1,0:T(8,128)(2,1)} %out_w_ref.1, f32[1,128]{1,0:T(1,128)} %bitcast.7, bf16[2,128,512]{2,1,0:T(8,128)(2,1)} %up_ref.1, bf16[512,128]{1,0:T(8,128)(2,1)} %down_ref.1), custom_call_target="tpu_custom_call" | custom-call | tf_op jit(solution)/shard_map/fused/pallas_call | solution.py:346
  136.6 2.1 %copy.9 = bf16[28,112,128]{2,1,0:T(8,128)(2,1)} copy(bf16[28,112,128]{2,1,0:T(8,128)(2,1)} %bitcast.4) | data formatting | bytes 1605632

commit v4 on v3

--- a/solution.py
+++ b/solution.py
@@ -94,8 +94,8 @@
     n_row, n_col, rows, cols,
     x_ref, gains_ref, proj_ref, out_w_ref, tgain_ref, up_ref, down_ref, o_ref,
     turned, gate, mid, summed, lefts, rights, outs,
-    send_a, recv_a, send_b, recv_b, send_c, recv_c, send_d, recv_d,
-    ssem_a, rsem_a, ssem_b, rsem_b, ssem_c, rsem_c, ssem_d, rsem_d,
+    send_l, recv_l, send_r, recv_r, send_b, recv_b, send_c, recv_c, send_d, recv_d,
+    ssem_l, rsem_l, ssem_r, rsem_r, ssem_b, rsem_b, ssem_c, rsem_c, ssem_d, rsem_d,
 ):
     n = n_row * n_col
     cells = rows * cols
@@ -108,7 +108,10 @@
     me = row * n_col + col
     f32, bf16 = jnp.float32, jnp.bfloat16
     starts = list(range(0, cells, step))
-    padded = send_a.shape[2]
+    padded = send_c.shape[2]
+    wide = 2 * each
+    some_rows = all_rows // 2
+    lane_wide = lax.broadcasted_iota(jnp.int32, (16, 128), 1)
     lane = lax.broadcasted_iota(jnp.int32, (8, 128), 1)
 
     def place(s):
@@ -123,6 +126,13 @@
             return 0
 
         lax.fori_loop(0, h, one, 0)
+        lax.fori_loop(h + 1, n, one, 0)
+
+    def near(body):
+        def one(s, _):
+            body(s)
+            return 0
+
         lax.fori_loop(h + 1, n, one, 0)
 
     barrier = pltpu.get_barrier_semaphore()
@@ -138,7 +148,8 @@
     tail = cells - cells // 128 * 128
     if tail:
         zero = jnp.zeros((n, 16, 128), bf16)
-        send_a[:, :, padded - 128 :] = zero
+        send_l[:, :, padded - 128 :] = zero[:h]
+        send_r[:, :, padded - 128 :] = zero[:h]
         send_c[:, :, padded - 128 :] = zero
 
     def remote(send, recv, ssem, rsem, k, lo, size, s, arriving):
@@ -165,7 +176,10 @@
                 turned[u, 256 * side + 128 : 256 * side + 256, :], flat, NT, preferred_element_type=f32
             )
             held = (jax.nn.sigmoid(scale) * value).astype(bf16)
-            send[:, each * side : each * side + each, lo : lo + size] = held.reshape(n, each, size)
+            if u == 0:
+                send[side][:, :, lo : lo + size] = held.reshape(h, wide, size)
+            else:
+                send[:, each * side : each * side + each, lo : lo + size] = held.reshape(n, each, size)
 
     def send_chunk(k, send, recv, ssem, rsem):
         lo, size = span(k)
@@ -202,19 +216,114 @@
 
             peers(one)
 
+    def halved(send, recv, ssem, rsem, k, lo, size, s, arriving, every):
+        peer, source, where = place(s)
+        slot = source if arriving else me
+        return pltpu.make_async_remote_copy(
+            src_ref=send.at[lax.rem(peer, h), :, pl.ds(lo, size)],
+            dst_ref=recv.at[slot if every else lax.rem(slot, h), :, pl.ds(lo, size)],
+            send_sem=ssem.at[k, s], recv_sem=rsem.at[k, s],
+            device_id=where, device_id_type=pl.DeviceIdType.MESH,
+        )
+
+    lefts_ahead = (send_l, recv_l, ssem_l, rsem_l)
+    rights_ahead = (send_r, recv_r, ssem_r, rsem_r)
+    sums_back = (send_b, recv_b, ssem_b, rsem_b)
+
+    def unpack_side(ref, slot, source, k, held, span_rows, r):
+        lo, size = span(k)
+        base = lax.rem(source, n_col) * (wide * span_rows) + r * rows
+        tiles = [ref[slot, :, lo + at : lo + at + 128].astype(f32) for at in range(0, size, 128)]
+        for part in range(2):
+            mine = [t[8 * part : 8 * part + 8] for t in tiles]
+            for i in range(min(TALL, rows - TALL * k)):
+                value = jnp.where(lane < cols, shifted(mine, cols * i), 0.0)
+                held[pl.ds(base + 8 * part * span_rows + TALL * k + i, 8, stride=span_rows), :] = value
+
+    def unpack_left(ref, source, k):
+        r = lax.rem(source // n_col, n_row // 2)
+        unpack_side(ref, lax.rem(source, h), source, k, lefts, some_rows, r)
+
+    def unpack_right(ref, slot, source, k):
+        unpack_side(ref, slot, source, k, rights, all_rows, source // n_col)
+
+    def send_first(k):
+        lo, size = span(k)
+        peers(lambda s: halved(*rights_ahead, k, lo, size, s, False, True).start())
+        near(lambda s: halved(*lefts_ahead, k, lo, size, s, False, False).start())
+        unpack_left(send_l, me, k)
+        unpack_right(send_r, lax.rem(me, h), me, k)
+
+    def receive_first():
+        for k in range(4):
+            lo, size = span(k)
+
+            def one_left(s):
+                halved(*lefts_ahead, k, lo, size, s, True, False).wait_recv()
+                unpack_left(recv_l, place(s)[1], k)
+
+            def one_right(s):
+                halved(*rights_ahead, k, lo, size, s, True, True).wait_recv()
+                source = place(s)[1]
+                unpack_right(recv_r, source, source, k)
+
+            near(one_left)
+            peers(one_right)
+
+    def pack_wide(ref, dest, g):
+        r, q = lax.rem(dest // n_col, n_row // 2), lax.rem(dest, n_col)
+        base = q * (wide * some_rows) + r * rows * wide
+        for lo in range(2 * g * step, min(2 * g * step + 2 * step, padded), 128):
+            total = jnp.zeros((16, 128), f32)
+            for i in range(rows):
+                at = i * cols - lo
+                if at >= 128 or at + cols <= 0:
+                    continue
+                value = outs[pl.ds(pl.multiple_of(base + i * wide, 16), wide), :]
+                if at % 128:
+                    value = pltpu.roll(value, at % 128, 1)
+                total = jnp.where((lane_wide >= at) & (lane_wide < at + cols), value, total)
+            ref[lax.rem(dest, h), :, lo : lo + 128] = total.astype(bf16)
+
+    def part_of(g):
+        return 2 * g * step, min(2 * step, padded - 2 * g * step)
+
+    def give_first():
+        for g in range(2):
+
+            def one(s):
+                pack_wide(send_b, place(s)[0], g)
+                halved(*sums_back, g, *part_of(g), s, False, False).start()
+
+            near(one)
+        for g in range(2):
+            pack_wide(recv_b, me, g)
+
+    def take_first(g):
+        near(lambda s: halved(*sums_back, g, *part_of(g), s, True, False).wait_recv())
+        lo, size = part_of(g)
+        for at in range(lo, lo + size, 128):
+            keep = min(128, cells - at)
+            piece = recv_b[:, :, at : at + 128].astype(f32).reshape(h * wide, 128).T
+            summed[at : at + keep, :] = piece[:keep]
+
     def channel(held, q, c, offset, size):
         at = pl.multiple_of(q * (each * all_rows) + c * all_rows + offset, 8)
         return held[pl.ds(at, size), :]
 
     def outgoing(c, _):
-        left = [channel(lefts, q, c, 0, all_rows).astype(bf16) for q in range(n_col)]
+        left = []
+        for q in range(n_col):
+            at = pl.multiple_of(q * (wide * some_rows) + c * some_rows, 8)
+            left.append(lefts[pl.ds(at, some_rows), :].astype(bf16))
         for jq in range(n_col):
             total = None
             for q in range(n_col):
-                right = channel(rights, q, c, jq * cols, 128).astype(bf16)
+                at = pl.multiple_of(q * (wide * all_rows) + c * all_rows + jq * cols, 8)
+                right = rights[pl.ds(at, 128), :].astype(bf16)
                 term = lax.dot_general(left[q], right, NT, preferred_element_type=f32)
                 total = term if total is None else total + term
-            outs[pl.ds(jq * (each * all_rows) + c, all_rows, stride=each), :] = total
+            outs[pl.ds(jq * (wide * some_rows) + c, some_rows, stride=wide), :] = total
         return 0
 
     def incoming(c, _):
@@ -278,28 +387,26 @@
     def bounds(k):
         return starts[k], min(step, cells - starts[k])
 
-    ahead_a = (send_a, recv_a, ssem_a, rsem_a)
-    back_a = (send_b, recv_b, ssem_b, rsem_b)
     ahead_b = (send_c, recv_c, ssem_c, rsem_c)
     back_b = (send_d, recv_d, ssem_d, rsem_d)
     for k in range(4):
         lo, size = bounds(k)
-        prepare(0, x_ref[lo : lo + size, :].astype(f32), lo, size, send_a)
+        prepare(0, x_ref[lo : lo + size, :].astype(f32), lo, size, (send_l, send_r))
         if k == 0:
             pl.semaphore_wait(barrier, n - 1)
-        send_chunk(k, *ahead_a)
-    receive((0, 1, 2, 3), *ahead_a)
-    lax.fori_loop(0, each, outgoing, 0)
-    give_back(*back_a)
+        send_first(k)
+    receive_first()
+    lax.fori_loop(0, wide, outgoing, 0)
+    give_first()
     for g in range(2):
-        take_back(g, *back_a)
-        for k in (g, g + 2):
+        take_first(g)
+        for k in (2 * g, 2 * g + 1):
             lo, size = bounds(k)
             held = finish(0, x_ref[lo : lo + size, :], lo, size)
             mid[lo : lo + size, :] = held
             prepare(1, held.astype(f32), lo, size, send_c)
             send_chunk(k, *ahead_b)
-    receive((0, 2, 1, 3), *ahead_b)
+    receive((0, 1, 2, 3), *ahead_b)
     lax.fori_loop(0, each, incoming, 0)
     give_back(*back_b)
 
@@ -321,14 +428,20 @@
             lax.fori_loop(lo // last, (lo + size) // last, transition, 0)
 
     def drain(s):
-        for held in (ahead_a, ahead_b):
-            for k in range(4):
-                lo, size = span(k)
-                remote(*held, k, lo, size, s, True).wait_send()
-        for held in (back_a, back_b):
-            for g in range(2):
-                remote(*held, g, g * step, step, s, True).wait_send()
-
+        for k in range(4):
+            lo, size = span(k)
+            halved(*rights_ahead, k, lo, size, s, True, True).wait_send()
+            remote(*ahead_b, k, lo, size, s, True).wait_send()
+        for g in range(2):
+            remote(*back_b, g, g * step, step, s, True).wait_send()
+
+    def drain_near(s):
+        for k in range(4):
+            halved(*lefts_ahead, k, *span(k), s, True, False).wait_send()
+        for g in range(2):
+            halved(*sums_back, g, *part_of(g), s, True, False).wait_send()
+
+    near(drain_near)
     peers(drain)
 
 
@@ -340,6 +453,8 @@
     ahead = pltpu.VMEM((n, 16, up128(cells)), jnp.bfloat16)
     back = pltpu.VMEM((n, 16, 2 * TALL * cols), jnp.bfloat16)
     panel = pltpu.VMEM((n_col * 8 * n_row * rows + 16, 128), jnp.float32)
+    panel_big = pltpu.VMEM((n_col * 16 * n_row * rows + 16, 128), jnp.float32)
+    ahead_half = pltpu.VMEM((n // 2, 16, up128(cells)), jnp.bfloat16)
     many = pltpu.SemaphoreType.DMA((4, n))
     few = pltpu.SemaphoreType.DMA((2, n))
     whole = pl.BlockSpec(memory_space=pltpu.VMEM)
@@ -353,9 +468,9 @@
             pltpu.VMEM((cells, width), jnp.float32),
             pltpu.VMEM((cells, width), jnp.bfloat16),
             pltpu.VMEM((cells, width), jnp.float32),
-            panel, panel, panel,
-            ahead, ahead, back, back, ahead, ahead, back, back,
-            many, many, few, few, many, many, few, few,
+            panel, panel_big, panel,
+            ahead_half, ahead_half, ahead_half, ahead, ahead_half, ahead_half, ahead, ahead, back, back,
+            many, many, many, many, few, few, many, many, few, few,
         ],
         compiler_params=pltpu.CompilerParams(
             collective_id=4, has_side_effects=True, vmem_limit_bytes=56 * 1024 * 1024
@@ -379,7 +494,7 @@
     cells = rows * cols
     each = width // n
     square = n_row * rows == n_col * cols
-    if each == 8 and width == 128 and square and n % 2 == 0 and cols % 16 == 0 and rows in (28, 32):
+    if each == 8 and width == 128 and square and n_row % 2 == 0 and cols % 16 == 0 and rows in (28, 32):
         return fused(n_row, n_col, pair, tri_gains, tri_proj, tri_out, trans_gain, trans_up, trans_down)
 
     def update(pair, gains, weights, out_weight, spec, cid):

time: 139 us -> 133 us (0.957)
  Pallas kernels: 137 us -> 131 us
    pallas_call x1, Pallas kernels: 137 us -> 131 us  [fused(): pl.pallas_call(functools.partial(fused_kernel, n_row, n_col, rows, cols),...]
where the time goes in v4:
time: 133 us
  Pallas kernels  131 us (98%)
  local copies, waits for them, and re-layouts  2.08 us (2%)
    pallas_call x1, Pallas kernels, fused(): pl.pallas_call(functools.partial(fused_kernel, n_row, n_col, rows, cols),...  131 us

profile of v4, /device:TPU:0, one launch (start us, length us, event | category | flops | bytes accessed | tf_op | source)
XLA Modules:
  0.0 133.0 jit_solution(14951280165857380115)
XLA Ops:
  0.0 130.9 %fused.1 = bf16[3136,128]{1,0:T(8,128)(2,1)} custom-call(bf16[3136,128]{1,0:T(8,128)(2,1)} %bitcast.5, f32[4,128]{1,0:T(4,128)} %bitcast.6, bf16[2,5,128,128]{3,2,1,0:T(8,128)(2,1)} %proj_ref.1, bf16[2,128,128]{2,1,0:T(8,128)(2,1)} %out_w_ref.1, f32[1,128]{1,0:T(1,128)} %bitcast.7, bf16[2,128,512]{2,1,0:T(8,128)(2,1)} %up_ref.1, bf16[512,128]{1,0:T(8,128)(2,1)} %down_ref.1), custom_call_target="tpu_custom_call" | custom-call | tf_op jit(solution)/shard_map/fused/pallas_call | solution.py:461
  130.9 2.1 %copy.9 = bf16[28,112,128]{2,1,0:T(8,128)(2,1)} copy(bf16[28,112,128]{2,1,0:T(8,128)(2,1)} %bitcast.4) | data formatting | bytes 1605632

commit v5 on v4

--- a/solution.py
+++ b/solution.py
@@ -336,18 +336,23 @@
                 outs[pl.ds(at, cols, stride=each), :] = total
         return 0
 
+    def fold(g):
+        tall = (rows - 2 * TALL) // 2 if g else TALL
+        return tall, -(-tall * cols // 128) * 128
+
     def pack(ref, dest, g):
         r, q = dest // n_col, lax.rem(dest, n_col)
         base = q * (each * all_rows) + r * rows * each
-        for t in range(step // 128):
+        tall, width = fold(g)
+        for t in range(width // 128):
             parts = []
-            for k in (g, g + 2):
+            for half in range(2):
                 total = jnp.zeros((8, 128), f32)
-                for i in range(min(TALL, rows - TALL * k)):
+                for i in range(tall):
                     at = i * cols - 128 * t
                     if at >= 128 or at + cols <= 0:
                         continue
-                    spot = pl.multiple_of(base + (TALL * k + i) * each, 8)
+                    spot = pl.multiple_of(base + (2 * TALL * g + half * tall + i) * each, 8)
                     value = outs[pl.ds(spot, each), :]
                     if at % 128:
                         value = pltpu.roll(value, at % 128, 1)
@@ -361,20 +366,21 @@
 
             def one(s):
                 pack(send, place(s)[0], g)
-                remote(send, recv, ssem, rsem, g, g * step, step, s, False).start()
+                remote(send, recv, ssem, rsem, g, g * step, fold(g)[1], s, False).start()
 
             peers(one)
         for g in range(2):
             pack(recv, me, g)
 
     def take_back(g, send, recv, ssem, rsem):
-        peers(lambda s: remote(send, recv, ssem, rsem, g, g * step, step, s, True).wait_recv())
-        for t in range(step // 128):
+        peers(lambda s: remote(send, recv, ssem, rsem, g, g * step, fold(g)[1], s, True).wait_recv())
+        tall, width = fold(g)
+        for t in range(width // 128):
             lo = g * step + 128 * t
             tile = recv[:, :, lo : lo + 128].astype(f32)
             for half in range(2):
-                at = (g + 2 * half) * step + 128 * t
-                keep = min(128, cells - at)
+                at = (2 * TALL * g + half * tall) * cols + 128 * t
+                keep = min(128, tall * cols - 128 * t)
                 if keep > 0:
                     piece = tile[:, each * half : each * half + each, :].reshape(n * each, 128).T
                     summed[at : at + keep, :] = piece[:keep]
@@ -423,7 +429,7 @@
 
     for g in range(2):
         take_back(g, *back_b)
-        for k in (g, g + 2):
+        for k in (2 * g, 2 * g + 1):
             lo, size = bounds(k)
             lax.fori_loop(lo // last, (lo + size) // last, transition, 0)
 
@@ -433,7 +439,7 @@
             halved(*rights_ahead, k, lo, size, s, True, True).wait_send()
             remote(*ahead_b, k, lo, size, s, True).wait_send()
         for g in range(2):
-            remote(*back_b, g, g * step, step, s, True).wait_send()
+            remote(*back_b, g, g * step, fold(g)[1], s, True).wait_send()
 
     def drain_near(s):
         for k in range(4):

time: 133 us -> 132 us (level)
  no operation moved by 1% of the time
where the time goes in v5:
time: 132 us
  Pallas kernels  130 us (98%)
  local copies, waits for them, and re-layouts  2.08 us (2%)
    pallas_call x1, Pallas kernels, fused(): pl.pallas_call(functools.partial(fused_kernel, n_row, n_col, rows, cols),...  130 us

profile of v5, /device:TPU:0, one launch (start us, length us, event | category | flops | bytes accessed | tf_op | source)
XLA Modules:
  0.0 131.9 jit_solution(10102244531590834164)
XLA Ops:
  0.0 129.8 %fused.1 = bf16[3136,128]{1,0:T(8,128)(2,1)} custom-call(bf16[3136,128]{1,0:T(8,128)(2,1)} %bitcast.5, f32[4,128]{1,0:T(4,128)} %bitcast.6, bf16[2,5,128,128]{3,2,1,0:T(8,128)(2,1)} %proj_ref.1, bf16[2,128,128]{2,1,0:T(8,128)(2,1)} %out_w_ref.1, f32[1,128]{1,0:T(1,128)} %bitcast.7, bf16[2,128,512]{2,1,0:T(8,128)(2,1)} %up_ref.1, bf16[512,128]{1,0:T(8,128)(2,1)} %down_ref.1), custom_call_target="tpu_custom_call" | custom-call | tf_op jit(solution)/shard_map/fused/pallas_call | solution.py:467
  129.9 2.1 %copy.9 = bf16[28,112,128]{2,1,0:T(8,128)(2,1)} copy(bf16[28,112,128]{2,1,0:T(8,128)(2,1)} %bitcast.4) | data formatting | bytes 1605632
